TPU v7x, 256 devices: a whole 4x4x8 slice. The times are simulated.
256 devices in a mesh: dp: 16 (over y, z_lo, core), tensor: 16 (over z_hi, x).
Axes of the slice: x: 4, y: 4, z: 8 (z_hi: 4, z_lo: 2; z = z_hi * 2 + z_lo), core: 2. Of those that a mesh axis runs over, the one named last changes fastest.
Arguments:
- query: bfloat16 [6144, 8192], P('dp', 'tensor'), may hold values from -140 to 140
- keys: bfloat16 [6144, 1024], P('dp'), may hold values from -6 to 6
- values: bfloat16 [6144, 1024], P('dp'), may hold values from -6 to 6
- out_grad: bfloat16 [6144, 8192], P(('dp', 'tensor')), may hold values from -24 to 24
- lengths: int32 [48], replicated, may hold values from 1 to 128, 3840 in all
- order: int32 [48], replicated, may hold values from 0 to 47, each once
Outputs:
- importance: float32 [8192, 8192], P('dp', 'tensor')
Inputs may be any that keep to these rules, and one draw needn't show every extreme that they name: `lengths`: the largest is exactly 128, and they sum to 3840. `order`: a permutation of the sequences over the slots.
All inputs are finite; a program needn't handle non-finite values.
Results may differ from a plain program's by a relative error of at most 0.0015.
Values may be sent and summed in bfloat16 or wider, within the bound.
A program may use at most 256 MiB of HBM per device.

v0:
```python
import math

import jax
import jax.numpy as jnp
from jax import lax
from jax.sharding import PartitionSpec as P

HEADS = 64
KV_HEADS = 8
HEAD_DIM = 128
SLOT_LEN = 128
SLOTS = 3


NEGATIVE_FILL = -1e30


def attend_slot(slot_query, slot_keys, slot_values, length, first_head, sharing):
    per_device = slot_query.shape[1] // HEAD_DIM
    row_index = jnp.arange(slot_query.shape[0], dtype=jnp.int32)[:, None]
    col_index = jnp.arange(slot_keys.shape[0], dtype=jnp.int32)[None, :]
    allowed = (col_index <= row_index) & (col_index < length)
    score_scale = 1.0 / math.sqrt(HEAD_DIM)
    pieces = []
    for head_pos in range(per_device):
        kv_start = (first_head + head_pos) // sharing * HEAD_DIM
        key_head = lax.dynamic_slice_in_dim(slot_keys, kv_start, HEAD_DIM, 1)
        value_head = lax.dynamic_slice_in_dim(slot_values, kv_start, HEAD_DIM, 1)
        query_head = slot_query[:, head_pos * HEAD_DIM : (head_pos + 1) * HEAD_DIM]
        scores = (
            lax.dot_general(
                query_head, key_head, (((1,), (1,)), ((), ())), preferred_element_type=jnp.float32
            )
            * score_scale
        )
        scores = jnp.where(allowed, scores, NEGATIVE_FILL)
        peak = jnp.max(scores, axis=1, keepdims=True)
        raised = jnp.exp(scores - peak)
        probs = (raised / jnp.sum(raised, axis=1, keepdims=True)).astype(jnp.bfloat16)
        pieces.append(jnp.dot(probs, value_head, preferred_element_type=jnp.float32))
    mixed = jnp.concatenate(pieces, axis=1)
    return jnp.where(row_index < length, mixed, 0.0).astype(jnp.bfloat16)


def slot_gradient(grad_cols, attention):
    return lax.dot_general(
        grad_cols, attention, (((0,), (0,)), ((), ())), preferred_element_type=jnp.float32
    )


def squared_sum(grad_rows, attentions):
    summed = jnp.zeros((grad_rows.shape[1], attentions[0].shape[1]), jnp.float32)
    for slot_pos in range(len(attentions)):
        grad_cols = grad_rows[slot_pos * SLOT_LEN : (slot_pos + 1) * SLOT_LEN]
        gradient = slot_gradient(grad_cols, attentions[slot_pos])
        summed = summed + gradient * gradient
    return summed


def local(query, keys, values, out_grad, lengths, order):
    tensor_size = lax.axis_size("tensor")
    dp_size = lax.axis_size("dp")
    per_device = HEADS // tensor_size
    sharing = HEADS // KV_HEADS
    first_head = lax.axis_index("tensor") * per_device
    sequence_ids = jnp.arange(lengths.shape[0], dtype=jnp.int32)
    slot_order = lax.dynamic_slice_in_dim(order, lax.axis_index("dp") * SLOTS, SLOTS)
    matches = slot_order[:, None] == sequence_ids[None, :]
    slot_lengths = jnp.sum(jnp.where(matches, lengths[None, :], 0), axis=1)
    attentions = []
    for slot_pos in range(SLOTS):
        lower = slot_pos * SLOT_LEN
        upper = lower + SLOT_LEN
        attentions.append(
            attend_slot(
                query[lower:upper],
                keys[lower:upper],
                values[lower:upper],
                slot_lengths[slot_pos],
                first_head,
                sharing,
            )
        )
    normalize = 1.0 / (SLOTS * dp_size * SLOT_LEN)
    gathered = lax.all_gather(out_grad, "tensor", axis=0, tiled=True)
    term = squared_sum(gathered, attentions)
    importance = lax.psum_scatter(term, "dp", scatter_dimension=0, tiled=True) * normalize
    return importance


def solution(mesh):
    placed = (P("dp", "tensor"), P("dp", None), P("dp", None), P(("dp", "tensor"), None), P(), P())
    return jax.shard_map(
        local, mesh=mesh, in_specs=placed, out_specs=P("dp", "tensor"), check_vma=False
    )
```

profile of v0, /device:TPU:2, one launch (start us, length us, event | category | flops | bytes accessed | tf_op | source)
XLA Modules:
  0.0 342.1 jit_solution(15738183244105699471)
XLA Ops:
  6.5 0.7 all-gather.2.cloned.1.call-update
  7.3 0.7 dynamic_slice.75
  8.1 0.8 select_reduce_fusion
  11.5 1.2 fusion.146
  12.7 0.9 fusion.157
  13.7 0.9 fusion.158
  14.6 0.9 fusion.159
  15.6 0.9 fusion.160
  16.6 0.9 fusion.153
  17.6 0.9 fusion.154
  18.6 0.9 fusion.155
  19.6 0.9 fusion.156
  20.5 0.9 fusion.149
  21.5 0.9 fusion.150
  22.5 0.9 fusion.151
  23.5 0.9 fusion.152
  24.5 1.2 fusion.147
  28.1 82.0 %all-gather.2.cloned.1.call-done = bf16[384,8192]{1,0:T(8,128)(2,1)} async-done(((bf16[24,8192]{1,0:T(8,128)(2,1)}), bf16[384,8192]{1,0:T(8,128)(2,1)}) %all-gather.2.cloned.1.call-update) | async-done | bytes 6291472 | tf_op jit(solution)/shard_map/all_gather | solution.py:85
  110.2 9.7 %fusion.3 = f32[512,8192]{1,0:T(8,128)} fusion(bf16[384,8192]{1,0:T(8,128)(2,1)} %all-gather.2.cloned.1.call-done, bf16[128,128]{1,0:T(8,128)(2,1)S(1)} %fusion.96, bf16[128,128]{1,0:T(8,128)(2,1)S(1)} %fusion.101, bf16[128,128]{1,0:T(8,128)(2,1)S(1)} %fusion.106, bf16[128,128]{1,0:T(8,128)(2,1)S(1)} %fusion.111, pred[128]{0:T(512)(128)(4,1)S(1)} %iota_compare_fusion.4), kind=kOutput, calls=%fused_computation.4 | convolution fusion | flops 1074331648 | bytes 19005568 | tf_op jit(solution)/shard_map/dot_general | solution.py:46
  119.9 9.7 %fusion.1 = f32[512,8192]{1,0:T(8,128)} fusion(bf16[384,8192]{1,0:T(8,128)(2,1)} %all-gather.2.cloned.1.call-done, bf16[128,128]{1,0:T(8,128)(2,1)S(1)} %fusion.76, bf16[128,128]{1,0:T(8,128)(2,1)S(1)} %fusion.81, bf16[128,128]{1,0:T(8,128)(2,1)S(1)} %fusion.86, bf16[128,128]{1,0:T(8,128)(2,1)S(1)} %fusion.91, pred[128]{0:T(512)(128)(4,1)S(1)} %iota_compare_fusion.3), kind=kOutput, calls=%fused_computation.2 | convolution fusion | flops 1074331648 | bytes 19005568 | tf_op jit(solution)/shard_map/dot_general | solution.py:46
  129.6 19.4 %add_bitcast_fusion = f32[8192,512]{0,1:T(8,128)} fusion(f32[512,8192]{1,0:T(8,128)} %fusion.1, f32[512,8192]{1,0:T(8,128)} %fusion.3, bf16[384,8192]{1,0:T(8,128)(2,1)} %all-gather.2.cloned.1.call-done, bf16[128,128]{1,0:T(8,128)(2,1)S(1)} %fusion.56, bf16[128,128]{1,0:T(8,128)(2,1)S(1)} %fusion.61, bf16[128,128]{1,0:T(8,128)(2,1)S(1)} %fusion.66, ...), kind=kOutput, calls=%fused_computation | convolution fusion | flops 1095303168 | bytes 52560000 | tf_op jit(solution)/shard_map/dot_general | solution.py:46
  149.1 183.5 %reduce-scatter.2.cloned.1.call-done = f32[512,512]{0,1:T(8,128)} async-done(((f32[8192,512]{0,1:T(8,128)}), f32[512,512]{0,1:T(8,128)}) %reduce-scatter.2.cloned.1.call-update) | async-done | bytes 1048592 | tf_op jit(solution)/shard_map/reduce_scatter | solution.py:87
  332.6 1.3 broadcast_multiply_fusion
  333.9 1.3 copy.8
  (31 shorter events, 5.5 us)
Async XLA Ops:
  6.5 103.6 %all-gather.2.cloned.1.call-start = ((), (), s32[]{:S(2)}) async-start(), calls=%async_computation.1 | async-start | bytes 6684672 | tf_op jit(solution)/shard_map/all_gather | solution.py:85
  7.3 325.3 %reduce-scatter.2.cloned.1.call-start = ((), (), s32[]{:S(2)}) async-start(), calls=%async_computation.2 | async-start | bytes 17825792 | tf_op jit(solution)/shard_map/reduce_scatter | solution.py:87
Sparse Core Ops, SparseCore 0:
  9.8 100.3 all-gather.1
  149.2 183.3 reduce-scatter.1
where the time goes:
time: 343 us; the launch traced here: 342 us
  waiting for transfers between devices  266 us (78%)
  matrix products  52.5 us (15%)
  between operations  13.6 us (4%)
  local copies, waits for them, and re-layouts  5.08 us (1%)
  other arithmetic  4.6 us (1%)
    reduce_scatter x1, waiting for transfers between devices, local(): lax.psum_scatter(term, 'dp', scatter_dimension=0, tiled=True) * normalize  184 us
    all_gather x1, waiting for transfers between devices, local(): gathered = lax.all_gather(out_grad, 'tensor', axis=0, tiled=True)  82 us
    dot_general x3, matrix products, slot_gradient(): lax.dot_general(grad_cols, attention, (((0,), (0,)), ((), ())), preferred...  38.9 us
    dot_general x12, matrix products, attend_slot(): lax.dot_general(query_head, key_head, (((1,), (1,)), ((), ())), preferred...  11.3 us
  transfers between devices with their start and end apart: 2, of which 2 were waited for; matrix products, arithmetic and copies ran while one was open for 6% of the time, Pallas kernels for 0%

commit v1 on v0

v1 whole, which is shorter than its diff:
```python
import math

import jax
import jax.numpy as jnp
from jax import lax
from jax.experimental import pallas as pl
from jax.experimental.pallas import tpu as pltpu
from jax.sharding import PartitionSpec as P

HEADS = 64
KV_HEADS = 8
HEAD_DIM = 128
SLOT_LEN = 128
SLOTS = 3
NEGATIVE_FILL = -1e30

NX = 4
NZ = 4
NY = 4
GROUPS = 16
ROWS = SLOTS * SLOT_LEN
PIECE = 24
ZROWS = NX * PIECE
WIDTH = 128
FEATS = 512
CH = 2
NC = GROUPS // CH
MESH = pl.DeviceIdType.MESH


def kernel(
    lengths_ref, order_ref, q_ref, k_hbm, v_hbm, g_ref, out_ref,
    kbuf, vbuf, pk, r0, s1, gx, att, acc,
    kv_sem, x0_send, x0_recv, d_send, d_recv, z_send, z_recv, x_send, x_recv,
    a_send, a_recv, b_send, b_recv,
):
    d = lax.axis_index("dp")
    t = lax.axis_index("tensor")
    zh, x = t // NX, t % NX
    y, zl, c = d // 4, (d // 2) % 2, d % 2

    def at_x(step):
        return (x + step + NX) % NX

    def at_z(step):
        return (zh + step + NZ) % NZ

    def dp_of(dy, dz, dc):
        return ((y + dy) % NY) * 4 + ((zl + dz) % 2) * 2 + (c + dc) % 2

    def dev_x(step):
        return {"dp": d, "tensor": zh * NX + at_x(step)}

    def dev_z(step):
        return {"dp": d, "tensor": at_z(step) * NX + x}

    def dev_dp(dy, dz, dc):
        return {"dp": dp_of(dy, dz, dc), "tensor": t}

    def remote(src, dst, send, recv, device):
        return pltpu.make_async_remote_copy(
            src_ref=src, dst_ref=dst, send_sem=send, recv_sem=recv,
            device_id=device, device_id_type=MESH,
        )

    barrier = pltpu.get_barrier_semaphore()
    peers = [dev_x(s) for s in (1, 2, 3)] + [dev_z(1), dev_z(-1)]
    peers += [dev_dp(i // 4, (i // 2) % 2, i % 2) for i in range(1, GROUPS)]
    for peer in peers:
        pl.semaphore_signal(barrier, inc=1, device_id=peer, device_id_type=MESH)

    kv_cols = pl.ds(pl.multiple_of((t // 2) * HEAD_DIM, HEAD_DIM), HEAD_DIM)
    k_copy = pltpu.make_async_copy(k_hbm.at[:, kv_cols], kbuf, kv_sem.at[0])
    v_copy = pltpu.make_async_copy(v_hbm.at[:, kv_cols], vbuf, kv_sem.at[1])
    k_copy.start()
    v_copy.start()

    for xb in range(NX):
        for m in range(GROUPS // 2):
            parts = []
            for gg in (2 * m, 2 * m + 1):
                lo = (gg * NX + xb) * WIDTH
                parts.append(g_ref[:, lo : lo + WIDTH].astype(jnp.float32))
            both = jnp.concatenate(parts, axis=0)
            pk[xb, m * 2 * PIECE : (m + 1) * 2 * PIECE, :] = both.astype(jnp.bfloat16)

    pl.semaphore_wait(barrier, len(peers))

    sends = []

    def x0_copy(s):
        return remote(pk.at[at_x(s)], r0.at[x], x0_send.at[s - 1], x0_recv.at[s - 1], dev_x(s))

    for s in (1, 2, 3):
        x0_copy(s).start()
        sends.append(x0_copy(s))
    r0[x] = pk[x]

    k_copy.wait()
    v_copy.wait()
    key_index = lax.broadcasted_iota(jnp.int32, (SLOT_LEN, SLOT_LEN), 0)
    row_index = lax.broadcasted_iota(jnp.int32, (SLOT_LEN, SLOT_LEN), 1)
    scale = 1.0 / math.sqrt(HEAD_DIM)
    for s in range(SLOTS):
        length = lengths_ref[order_ref[d * SLOTS + s]]
        rows = slice(s * SLOT_LEN, (s + 1) * SLOT_LEN)
        allowed = (key_index <= row_index) & (key_index < length)
        live = row_index < length
        keys = kbuf[rows, :]
        values_t = vbuf[rows, :].astype(jnp.float32).T.astype(jnp.bfloat16)
        for h in range(FEATS // HEAD_DIM):
            feats = slice(h * HEAD_DIM, (h + 1) * HEAD_DIM)
            scores = lax.dot_general(
                keys, q_ref[rows, feats], (((1,), (1,)), ((), ())),
                preferred_element_type=jnp.float32,
            ) * scale
            scores = jnp.where(allowed, scores, NEGATIVE_FILL)
            peak = jnp.max(scores, axis=0, keepdims=True)
            raised = jnp.exp(scores - peak)
            probs = (raised / jnp.sum(raised, axis=0, keepdims=True)).astype(jnp.bfloat16)
            mixed = jnp.dot(values_t, probs, preferred_element_type=jnp.float32)
            att[0, feats, rows] = jnp.where(live, mixed, 0.0).astype(jnp.bfloat16)

    def a_copy(src, dst, n, dy, dz):
        return remote(att.at[2 * src], att.at[2 * dst], a_send.at[n], a_recv.at[dst], dev_dp(dy, dz, 0))

    def b_copy(q):
        return remote(att.at[2 * q], att.at[2 * q + 1], b_send.at[q], b_recv.at[q], dev_dp(0, 0, 1))

    def go(copy):
        copy.start()
        sends.append(copy)

    def a_wait(q):
        a_copy(q, q, 0, 0, 1).wait_recv()

    go(a_copy(0, 1, 0, 0, 1))
    go(a_copy(0, 6, 1, 1, 0))
    go(a_copy(0, 2, 2, 3, 0))
    go(b_copy(0))

    for s in (1, 2, 3):
        remote(pk.at[x], r0.at[at_x(-s)], x0_send.at[s - 1], x0_recv.at[s - 1], dev_x(s)).wait_recv()
    for m in range(GROUPS // 2):
        parts = [r0[xb, m * 2 * PIECE : (m + 1) * 2 * PIECE, :].astype(jnp.float32) for xb in range(NX)]
        for e in range(2):
            rows = jnp.concatenate([p[e * PIECE : (e + 1) * PIECE] for p in parts], axis=0)
            s1[2 * m + e] = rows.astype(jnp.bfloat16)

    own_rows = pl.ds(pl.multiple_of(zh * ZROWS, ZROWS), ZROWS)

    for i in range(1, GROUPS):
        dy, dz, dc = i // 4, (i // 2) % 2, i % 2
        j = ((NY - dy) % NY) * 4 + dz * 2 + dc
        go(remote(s1.at[dp_of(dy, dz, dc)], gx.at[x, j, own_rows], d_send.at[i], d_recv.at[j], dev_dp(dy, dz, dc)))
    gx[x, 0, own_rows, :] = s1[d]

    def z_piece(q, step):
        rows = pl.ds(pl.multiple_of(at_z(step) * ZROWS, ZROWS), ZROWS)
        return gx.at[x, pl.ds(q * CH, CH), rows]

    def z_copy(q, kind):
        if kind == 0:
            piece, step = z_piece(q, 0), 1
        elif kind == 1:
            piece, step = z_piece(q, 0), -1
        elif q % 2 == 0:
            piece, step = z_piece(q, -1), 1
        else:
            piece, step = z_piece(q, 1), -1
        return remote(piece, piece, z_send.at[kind, q], z_recv.at[kind, q], dev_z(step))

    def z_wait(q, kind):
        piece = z_piece(q, (-1, 1, 2)[kind])
        remote(piece, piece, z_send.at[kind, q], z_recv.at[kind, q], dev_z(1)).wait_recv()

    def x_piece(q, step):
        return gx.at[at_x(step), pl.ds(q * CH, CH)]

    def x_copy(q, kind):
        if kind == 0:
            piece, step = x_piece(q, 0), 1
        elif kind == 1:
            piece, step = x_piece(q, 0), -1
        elif q % 2 == 0:
            piece, step = x_piece(q, -1), 1
        else:
            piece, step = x_piece(q, 1), -1
        return remote(piece, piece, x_send.at[kind, q], x_recv.at[kind, q], dev_x(step))

    def x_wait(q, kind):
        piece = x_piece(q, (-1, 1, 2)[kind])
        remote(piece, piece, x_send.at[kind, q], x_recv.at[kind, q], dev_x(1)).wait_recv()

    def add_block(xb, i):
        total = None
        for s in range(SLOTS):
            rows = slice(s * SLOT_LEN, (s + 1) * SLOT_LEN)
            gradient = jnp.dot(att[i, :, rows], gx[xb, i, rows, :], preferred_element_type=jnp.float32)
            square = gradient * gradient
            total = square if total is None else total + square
        acc[xb] += total

    def add_blocks(q, first, count):
        def body(n, carry):
            add_block((x + first + n // CH) % NX, q * CH + n % CH)
            return carry

        lax.fori_loop(0, count * CH, body, 0)

    def z_own(q):
        if q == 0:
            d_wait(1)
        else:
            for i in range(q * CH, (q + 1) * CH):
                d_wait(i)
        go(z_copy(q, 0))
        go(z_copy(q, 1))

    def d_wait(i):
        remote(s1.at[0], gx.at[x, i, own_rows], d_send.at[i], d_recv.at[i], dev_dp(0, 0, 1)).wait_recv()

    acc[...] = jnp.zeros_like(acc)
    z_own(0)
    z_own(1)
    a_events = {
        0: [1],
        1: [6, 3],
        2: [2, 7],
        3: [4],
        4: [5],
    }

    def a_event(q):
        a_wait(q)
        if q == 1:
            go(a_copy(1, 7, 3, 1, 0))
            go(a_copy(1, 3, 4, 3, 0))
        if q == 6:
            go(a_copy(6, 4, 5, 1, 0))
        if q == 3:
            go(a_copy(3, 5, 6, 3, 0))
        go(b_copy(q))

    for n in range(NC + 3):
        if n < NC:
            z_wait(n, 0)
            z_wait(n, 1)
            go(z_copy(n, 2))
            if n + 2 < NC:
                z_own(n + 2)
        if 0 <= n - 1 < NC:
            z_wait(n - 1, 2)
            go(x_copy(n - 1, 0))
            go(x_copy(n - 1, 1))
        for q in a_events.get(n, ()):
            a_event(q)
        if 0 <= n - 2 < NC:
            x_wait(n - 2, 0)
            x_wait(n - 2, 1)
            go(x_copy(n - 2, 2))
            b_copy(n - 2).wait_recv()
            add_blocks(n - 2, 3, 3)
        if 0 <= n - 3 < NC:
            x_wait(n - 3, 2)
            add_blocks(n - 3, 2, 1)

    for xb in range(NX):
        out_ref[xb * WIDTH : (xb + 1) * WIDTH, :] = acc[xb].T

    for copy in sends:
        copy.wait_send()


def local(query, keys, values, out_grad, lengths, order):
    vmem = pl.BlockSpec(memory_space=pltpu.VMEM)
    smem = pl.BlockSpec(memory_space=pltpu.SMEM)
    hbm = pl.BlockSpec(memory_space=pl.ANY)
    bf16 = jnp.bfloat16
    dma = pltpu.SemaphoreType.DMA
    summed = pl.pallas_call(
        kernel,
        out_shape=jax.ShapeDtypeStruct((NX * WIDTH, FEATS), jnp.float32),
        in_specs=[smem, smem, vmem, hbm, hbm, vmem],
        out_specs=vmem,
        scratch_shapes=[
            pltpu.VMEM((ROWS, HEAD_DIM), bf16),
            pltpu.VMEM((ROWS, HEAD_DIM), bf16),
            pltpu.VMEM((NX, GROUPS * PIECE, WIDTH), bf16),
            pltpu.VMEM((NX, GROUPS * PIECE, WIDTH), bf16),
            pltpu.VMEM((GROUPS, ZROWS, WIDTH), bf16),
            pltpu.VMEM((NX, GROUPS, ROWS, WIDTH), bf16),
            pltpu.VMEM((GROUPS, FEATS, ROWS), bf16),
            pltpu.VMEM((NX, FEATS, WIDTH), jnp.float32),
            dma((2,)),
            dma((3,)), dma((3,)),
            dma((GROUPS,)), dma((GROUPS,)),
            dma((3, NC)), dma((3, NC)),
            dma((3, NC)), dma((3, NC)),
            dma((8,)), dma((8,)),
            dma((8,)), dma((8,)),
        ],
        compiler_params=pltpu.CompilerParams(
            collective_id=0, has_side_effects=True, vmem_limit_bytes=44 * 1024 * 1024
        ),
        cost_estimate=pl.CostEstimate(
            flops=2 * 48 * 128 * 512 * 512, bytes_accessed=4 * 1024 * 1024, transcendentals=12 * 128 * 128
        ),
    )(lengths, order, query, keys, values, out_grad)
    return summed * (1.0 / (GROUPS * ROWS))


def solution(mesh):
    placed = (P("dp", "tensor"), P("dp", None), P("dp", None), P(("dp", "tensor"), None), P(), P())
    return jax.shard_map(
        local, mesh=mesh, in_specs=placed, out_specs=P("dp", "tensor"), check_vma=False
    )
```

time: 343 us -> 101 us (0.29)
  waiting for transfers between devices: 266 us -> 0 us
  Pallas kernels: 0 us -> 92.4 us
  matrix products: 52.5 us -> 0 us
  between operations: 13.6 us -> 0.02 us
  other arithmetic: 4.6 us -> 1.08 us
    reduce_scatter x1 -> x0, waiting for transfers between devices: 184 us -> none  [local(): lax.psum_scatter(term, 'dp', scatter_dimension=0, tiled=True) * normalize]
    pallas_call x0 -> x1, Pallas kernels: none -> 92.4 us  [local(): pl.pallas_call(kernel, out_shape=jax.ShapeDtypeStruct((NX * WIDTH, FEATS)...]
    all_gather x1 -> x0, waiting for transfers between devices: 82 us -> none  [local(): gathered = lax.all_gather(out_grad, 'tensor', axis=0, tiled=True)]
    dot_general x27 -> x0, matrix products: 52.5 us -> none  [the longest x3 38.9 us: slot_gradient(): lax.dot_general(grad_cols, attention, (((0,), (0,)), ((), ())), preferred...]
    unnamed x0 -> x12, local copies, waits for them, and re-layouts: none -> 5.57 us
  transfers between devices with their start and end apart: 2 -> 0, of which waited for: 2 -> 0; matrix products, arithmetic and copies ran while one was open for 6% -> 0% of each run, Pallas kernels for 0% -> 0%
where the time goes in v1:
time: 101 us; the launch traced here: 99 us
  Pallas kernels  92.4 us (91%)
  local copies, waits for them, and re-layouts  5.57 us (6%)
  other arithmetic  1.08 us (1%)
    pallas_call x1, Pallas kernels, local(): pl.pallas_call(kernel, out_shape=jax.ShapeDtypeStruct((NX * WIDTH, FEATS)...  92.4 us
    unnamed x12, local copies, waits for them, and re-layouts  5.57 us

profile of v1, /device:TPU:2, one launch (start us, length us, event | category | flops | bytes accessed | tf_op | source)
XLA Modules:
  0.0 99.0 jit_solution(11954598148168209663)
XLA Ops:
  0.0 0.0 copy-start
  0.0 1.1 %copy-done = bf16[384,1024]{1,0:T(8,128)(2,1)S(1)} copy-done((bf16[384,1024]{1,0:T(8,128)(2,1)S(1)}, bf16[384,1024]{1,0:T(8,128)(2,1)}, u32[]{:S(2)}) %copy-start) | copy-done | bytes 786456
  1.1 0.0 copy-start.1
  1.1 1.1 %copy-done.1 = bf16[384,1024]{1,0:T(8,128)(2,1)S(1)} copy-done((bf16[384,1024]{1,0:T(8,128)(2,1)S(1)}, bf16[384,1024]{1,0:T(8,128)(2,1)}, u32[]{:S(2)}) %copy-start.1) | copy-done | bytes 786456
  2.3 0.0 copy-start.2
  2.3 1.0 %copy-done.2 = bf16[384,512]{1,0:T(8,128)(2,1)S(1)} copy-done((bf16[384,512]{1,0:T(8,128)(2,1)S(1)}, bf16[384,512]{1,0:T(8,128)(2,1)}, u32[]{:S(2)}) %copy-start.2) | copy-done | bytes 393240
  3.3 0.0 copy-start.3
  3.3 1.0 %copy-done.3 = bf16[24,8192]{1,0:T(8,128)(2,1)S(1)} copy-done((bf16[24,8192]{1,0:T(8,128)(2,1)S(1)}, bf16[24,8192]{1,0:T(8,128)(2,1)}, u32[]{:S(2)}) %copy-start.3) | copy-done | bytes 393240
  4.3 0.0 copy-start.4
  4.3 0.7 copy-done.4
  4.9 0.0 copy-start.5
  4.9 0.7 copy-done.5
  5.6 92.4 %shard_map.64 = f32[512,512]{1,0:T(8,128)S(1)} custom-call(s32[48]{0:T(128)S(1)} %copy-done.4, s32[48]{0:T(128)S(1)} %copy-done.5, bf16[384,512]{1,0:T(8,128)(2,1)S(1)} %copy-done.2, bf16[384,1024]{1,0:T(8,128)(2,1)S(1)} %copy-done, bf16[384,1024]{1,0:T(8,128)(2,1)S(1)} %copy-done.1, bf16[24,8192]{1,0:T(8,128)(2,1)S(1)} %copy-done.3), custom_call_target="tpu_custom_call" | custom-call | flops 3221225472 | bytes 4194304 | tf_op jit(solution)/shard_map/pallas_call | solution.py:281
  97.9 1.1 %broadcast_multiply_fusion = f32[512,512]{1,0:T(8,128)} fusion(f32[512,512]{1,0:T(8,128)S(1)} %shard_map.64), kind=kLoop, calls=%fused_computation | loop fusion | flops 262144 | bytes 2097152 | tf_op jit(solution)/shard_map/mul | solution.py:310
Async XLA Ops:
  0.0 1.1 %copy-start = (bf16[384,1024]{1,0:T(8,128)(2,1)S(1)}, bf16[384,1024]{1,0:T(8,128)(2,1)}, u32[]{:S(2)}) copy-start(bf16[384,1024]{1,0:T(8,128)(2,1)} %k_hbm.1) | copy-start | bytes 2359300
  1.1 1.1 %copy-start.1 = (bf16[384,1024]{1,0:T(8,128)(2,1)S(1)}, bf16[384,1024]{1,0:T(8,128)(2,1)}, u32[]{:S(2)}) copy-start(bf16[384,1024]{1,0:T(8,128)(2,1)} %v_hbm.1) | copy-start | bytes 2359300
  2.3 1.0 %copy-start.2 = (bf16[384,512]{1,0:T(8,128)(2,1)S(1)}, bf16[384,512]{1,0:T(8,128)(2,1)}, u32[]{:S(2)}) copy-start(bf16[384,512]{1,0:T(8,128)(2,1)} %q_ref.1) | copy-start | bytes 1179652
  3.3 1.0 %copy-start.3 = (bf16[24,8192]{1,0:T(8,128)(2,1)S(1)}, bf16[24,8192]{1,0:T(8,128)(2,1)}, u32[]{:S(2)}) copy-start(bf16[24,8192]{1,0:T(8,128)(2,1)} %g_ref.1) | copy-start | bytes 1179652
  4.3 0.7 copy-start.4
  4.9 0.7 copy-start.5

commit v2 on v1

v2 whole, which is shorter than its diff:
```python
import math

import jax
import jax.numpy as jnp
from jax import lax
from jax.experimental import pallas as pl
from jax.experimental.pallas import tpu as pltpu
from jax.sharding import PartitionSpec as P

HEADS = 64
KV_HEADS = 8
HEAD_DIM = 128
SLOT_LEN = 128
SLOTS = 3
NEGATIVE_FILL = -1e30

NX = 4
NZ = 4
NY = 4
GROUPS = 16
ROWS = SLOTS * SLOT_LEN
PIECE = 24
ZROWS = NX * PIECE
WIDTH = 128
FEATS = 512
PARTS = (0, 2, 1, 3)
X_FIRST = (0, 1, 2)
DIRECT = (3, 4, 5, 6)
ORDER = (
    ("xo", 0), ("xo", 1), ("xo", 2), ("zo", 3), ("zo", 8), ("zo", 12), ("zo", 4), ("xp", 0),
    ("zo", 9), ("zo", 5), ("xp", 1), ("xp", 2), ("zo", 6), ("zp", 8), ("zo", 7), ("xo", 3),
    ("zp", 12), ("zo", 10), ("A", 0), ("zp", 9), ("zo", 11), ("xo", 4), ("xp", 3), ("xo", 5),
    ("xo", 8), ("xp", 4), ("xo", 6), ("zp", 7), ("zo", 13), ("zp", 10), ("zo", 14), ("xp", 5),
    ("xo", 12), ("A", 2), ("A", 6), ("c3", 4), ("c3", 5), ("xp", 8), ("c1", 4), ("xp", 6),
    ("c1", 5), ("A", 1), ("c3", 3), ("xp", 12), ("xo", 9), ("zp", 11), ("zo", 15), ("c1", 3),
    ("xo", 7), ("A", 4), ("c3", 8), ("zp", 13), ("zo", 0), ("c1", 8), ("xo", 10), ("c3", 12),
    ("zp", 14), ("zo", 1), ("c1", 12), ("zp", 15), ("xp", 9), ("xo", 11), ("zo", 2), ("c3", 9),
    ("xp", 7), ("xo", 13), ("A", 3), ("A", 7), ("c3", 6), ("c1", 6), ("xp", 10), ("c3", 7),
    ("zp", 0), ("xo", 14), ("c1", 9), ("xp", 11), ("c1", 7), ("zp", 1), ("xo", 15), ("xp", 13),
    ("c3", 13), ("A", 5), ("c3", 10), ("c1", 10), ("c3", 11), ("zp", 2), ("xp", 14), ("c3", 14),
    ("c1", 11), ("c4", 0), ("xp", 15), ("c3", 15), ("c1", 13), ("c1", 14), ("c4", 1), ("c4", 2),
    ("c1", 15),
)
MESH = pl.DeviceIdType.MESH


def kernel(
    lengths_hbm, order_hbm, q_hbm, k_hbm, v_hbm, g_hbm, out_ref,
    lengths_ref, order_ref, q_ref, g_ref, kbuf, vbuf, pk, r0, s1, gx, att, acc,
    kv_sem, x0_send, x0_recv, d_send, d_recv, z_send, z_recv, x_send, x_recv,
    a_send, a_recv, b_send, b_recv,
):
    d = lax.axis_index("dp")
    t = lax.axis_index("tensor")
    zh, x = t // NX, t % NX
    y, zl, c = d // 4, (d // 2) % 2, d % 2

    def at_x(step):
        return (x + step + NX) % NX

    def at_z(step):
        return (zh + step + NZ) % NZ

    def dp_of(dy, dz, dc):
        return ((y + dy) % NY) * 4 + ((zl + dz) % 2) * 2 + (c + dc) % 2

    def dev_x(step):
        return {"dp": d, "tensor": zh * NX + at_x(step)}

    def dev_z(step):
        return {"dp": d, "tensor": at_z(step) * NX + x}

    def dev_dp(dy, dz, dc):
        return {"dp": dp_of(dy, dz, dc), "tensor": t}

    def remote(src, dst, send, recv, device):
        return pltpu.make_async_remote_copy(
            src_ref=src, dst_ref=dst, send_sem=send, recv_sem=recv,
            device_id=device, device_id_type=MESH,
        )

    barrier = pltpu.get_barrier_semaphore()
    peers = [dev_x(s) for s in (1, 2, 3)] + [dev_z(s) for s in (1, 2, 3)]
    peers += [dev_dp(i // 4, (i // 2) % 2, i % 2) for i in range(1, GROUPS)]
    for peer in peers:
        pl.semaphore_signal(barrier, inc=1, device_id=peer, device_id_type=MESH)

    g_copy = pltpu.make_async_copy(g_hbm, g_ref, kv_sem.at[2])
    q_copy = pltpu.make_async_copy(q_hbm, q_ref, kv_sem.at[3])
    l_copy = pltpu.make_async_copy(lengths_hbm, lengths_ref, kv_sem.at[4])
    o_copy = pltpu.make_async_copy(order_hbm, order_ref, kv_sem.at[5])
    g_copy.start()
    kv_cols = pl.ds(pl.multiple_of((t // 2) * HEAD_DIM, HEAD_DIM), HEAD_DIM)
    k_copy = pltpu.make_async_copy(k_hbm.at[:, kv_cols], kbuf, kv_sem.at[0])
    v_copy = pltpu.make_async_copy(v_hbm.at[:, kv_cols], vbuf, kv_sem.at[1])
    k_copy.start()
    q_copy.start()
    v_copy.start()
    l_copy.start()
    o_copy.start()
    g_copy.wait()

    for i in range(0, GROUPS, 2):
        lanes = [dp_of(j // 4, (j // 2) % 2, j % 2) * FEATS for j in (i, i + 1)]
        for xb in range(NX):
            parts = []
            for lane in lanes:
                cols = pl.ds(pl.multiple_of(lane + xb * WIDTH, WIDTH), WIDTH)
                parts.append(g_ref[:, cols].astype(jnp.float32))
            both = jnp.concatenate(parts, axis=0)
            pk[xb, i * PIECE : (i + 2) * PIECE, :] = both.astype(jnp.bfloat16)

    pl.semaphore_wait(barrier, len(peers))

    sends = []

    def go(copy):
        copy.start()
        sends.append(copy)

    def x0_rows(dy):
        return pl.ds(dy * 4 * PIECE, 4 * PIECE)

    for dy in PARTS:
        for s in (1, 2, 3):
            go(remote(
                pk.at[at_x(s), x0_rows(dy)], r0.at[x, x0_rows(dy)],
                x0_send.at[s - 1, dy], x0_recv.at[s - 1, dy], dev_x(s),
            ))
    r0[x] = pk[x]
    acc[...] = jnp.zeros_like(acc)

    k_copy.wait()
    v_copy.wait()
    q_copy.wait()
    l_copy.wait()
    o_copy.wait()
    key_index = lax.broadcasted_iota(jnp.int32, (SLOT_LEN, SLOT_LEN), 0)
    row_index = lax.broadcasted_iota(jnp.int32, (SLOT_LEN, SLOT_LEN), 1)
    scale = 1.0 / math.sqrt(HEAD_DIM)
    for s in range(SLOTS):
        length = lengths_ref[order_ref[d * SLOTS + s]]
        rows = slice(s * SLOT_LEN, (s + 1) * SLOT_LEN)
        allowed = (key_index <= row_index) & (key_index < length)
        live = row_index < length
        keys = kbuf[rows, :]
        values_t = vbuf[rows, :].astype(jnp.float32).T.astype(jnp.bfloat16)
        for h in range(FEATS // HEAD_DIM):
            feats = slice(h * HEAD_DIM, (h + 1) * HEAD_DIM)
            scores = lax.dot_general(
                keys, q_ref[rows, feats], (((1,), (1,)), ((), ())),
                preferred_element_type=jnp.float32,
            ) * scale
            scores = jnp.where(allowed, scores, NEGATIVE_FILL)
            peak = jnp.max(scores, axis=0, keepdims=True)
            raised = jnp.exp(scores - peak)
            probs = (raised / jnp.sum(raised, axis=0, keepdims=True)).astype(jnp.bfloat16)
            mixed = jnp.dot(values_t, probs, preferred_element_type=jnp.float32)
            att[0, feats, rows] = jnp.where(live, mixed, 0.0).astype(jnp.bfloat16)

    def a_copy(src, dst, n, dy, dz):
        return remote(att.at[2 * src], att.at[2 * dst], a_send.at[n], a_recv.at[dst], dev_dp(dy, dz, 0))

    def b_copy(q):
        return remote(att.at[2 * q], att.at[2 * q + 1], b_send.at[q], b_recv.at[q], dev_dp(0, 0, 1))

    def a_wait(q):
        a_copy(q, q, 0, 0, 1).wait_recv()

    own_rows = pl.ds(pl.multiple_of(zh * ZROWS, ZROWS), ZROWS)

    for dy in PARTS:
        for s in (1, 2, 3):
            remote(
                pk.at[x, x0_rows(dy)], r0.at[at_x(-s), x0_rows(dy)],
                x0_send.at[s - 1, dy], x0_recv.at[s - 1, dy], dev_x(s),
            ).wait_recv()
        for i in range(dy * 4, dy * 4 + 4, 2):
            parts = [r0[xb, i * PIECE : (i + 2) * PIECE, :].astype(jnp.float32) for xb in range(NX)]
            for e in range(2):
                rows = jnp.concatenate([p[e * PIECE : (e + 1) * PIECE] for p in parts], axis=0)
                s1[i + e] = rows.astype(jnp.bfloat16)
        for i in range(dy * 4, dy * 4 + 4):
            if i == 0:
                gx[x, 0, own_rows, :] = s1[0]
                continue
            dz, dc = (i // 2) % 2, i % 2
            j = ((NY - dy) % NY) * 4 + dz * 2 + dc
            go(remote(s1.at[i], gx.at[x, j, own_rows], d_send.at[i], d_recv.at[j], dev_dp(dy, dz, dc)))

    def d_wait(i):
        remote(s1.at[i], gx.at[x, i, own_rows], d_send.at[i], d_recv.at[i], dev_dp(0, 0, 1)).wait_recv()

    def rows_of(start, size, kind):
        if kind < 2:
            return pl.ds(pl.multiple_of(start, 16), size)
        return pl.ds(pl.multiple_of(start + (kind - 2) * (size // 2), 16), size // 2)

    def z_piece(i, step, kind):
        if i in DIRECT:
            kind = 0
        rows = rows_of(at_z(step) * ZROWS, ZROWS, kind)
        return gx.at[:, i, rows] if i in X_FIRST else gx.at[x, i, rows]

    def x_piece(i, step, kind):
        rows = rows_of(zh * ZROWS, ZROWS, kind) if i in X_FIRST else rows_of(0, ROWS, kind)
        return gx.at[at_x(step), i, rows]

    def z_ring(i, kind, arriving):
        if i in DIRECT:
            held = (-1, 1, 2)[kind] if arriving else 0
            step = (1, -1, 2)[kind]
        else:
            held = (-1, 1, 2, 2)[kind] if arriving else (0, 0, -1, 1)[kind]
            step = (1, -1, 1, -1)[kind]
        part = z_piece(i, held, kind)
        return remote(part, part, z_send.at[kind, i], z_recv.at[kind, i], dev_z(step))

    def x_ring(i, kind, arriving):
        held = (-1, 1, 2, 2)[kind] if arriving else (0, 0, -1, 1)[kind]
        step = (1, -1, 1, -1)[kind]
        part = x_piece(i, held, kind)
        return remote(part, part, x_send.at[kind, i], x_recv.at[kind, i], dev_x(step))

    def add_block(xb, i):
        total = None
        for s in range(SLOTS):
            rows = slice(s * SLOT_LEN, (s + 1) * SLOT_LEN)
            gradient = jnp.dot(att[i, :, rows], gx[xb, i, rows, :], preferred_element_type=jnp.float32)
            square = gradient * gradient
            total = square if total is None else total + square
        acc[xb] += total

    def add_blocks(i, first, count):
        def body(n, carry):
            add_block((x + first + n) % NX, i)
            return carry

        lax.fori_loop(0, count, body, 0)

    waited = set()

    def need(kind, *at):
        if (kind, at) in waited:
            return
        waited.add((kind, at))
        if kind == "d":
            d_wait(*at)
        elif kind == "z":
            z_ring(*at, True).wait_recv()
        elif kind == "x":
            x_ring(*at, True).wait_recv()
        elif kind == "a":
            a_wait(*at)
        else:
            b_copy(*at).wait_recv()

    def need_z(i):
        for kind in range(3 if i in DIRECT else 4):
            need("z", i, kind)

    def need_d(i):
        if i > 0:
            need("d", i)

    def step(kind, i):
        if kind == "A":
            if i == 0:
                go(a_copy(0, 1, 0, 0, 1))
                go(a_copy(0, 6, 1, 1, 0))
                go(a_copy(0, 2, 2, 3, 0))
                go(a_copy(0, 4, 6, 2, 0))
            else:
                need("a", i)
            if i == 1:
                go(a_copy(1, 7, 3, 1, 0))
                go(a_copy(1, 3, 4, 3, 0))
                go(a_copy(1, 5, 5, 2, 0))
            go(b_copy(i))
        elif kind == "zo":
            if i in X_FIRST:
                for part in range(4):
                    need("x", i, part)
            else:
                need_d(i)
            for part in range(3 if i in DIRECT else 2):
                go(z_ring(i, part, False))
        elif kind == "zp":
            for part in range(2):
                need("z", i, part)
            for part in (2, 3):
                go(z_ring(i, part, False))
        elif kind == "xo":
            if i in X_FIRST:
                need_d(i)
            else:
                need_z(i)
            for part in range(2):
                go(x_ring(i, part, False))
        elif kind == "xp":
            for part in range(2):
                need("x", i, part)
            for part in (2, 3):
                go(x_ring(i, part, False))
        else:
            if i % 2:
                need("b", i // 2)
            if kind == "c4":
                need_z(i)
                add_blocks(i, 0, 4)
            elif kind == "c3":
                need("x", i, 0)
                need("x", i, 1)
                add_blocks(i, 3, 3)
            else:
                need("x", i, 2)
                need("x", i, 3)
                add_blocks(i, 2, 1)

    for kind, i in ORDER:
        step(kind, i)

    for xb in range(NX):
        out_ref[xb * WIDTH : (xb + 1) * WIDTH, :] = acc[xb].T * (1.0 / (GROUPS * ROWS))

    for copy in sends:
        copy.wait_send()


def local(query, keys, values, out_grad, lengths, order):
    vmem = pl.BlockSpec(memory_space=pltpu.VMEM)
    hbm = pl.BlockSpec(memory_space=pl.ANY)
    bf16 = jnp.bfloat16
    dma = pltpu.SemaphoreType.DMA
    summed = pl.pallas_call(
        kernel,
        out_shape=jax.ShapeDtypeStruct((NX * WIDTH, FEATS), jnp.float32),
        in_specs=[hbm] * 6,
        out_specs=vmem,
        scratch_shapes=[
            pltpu.SMEM(lengths.shape, jnp.int32),
            pltpu.SMEM(order.shape, jnp.int32),
            pltpu.VMEM(query.shape, bf16),
            pltpu.VMEM(out_grad.shape, bf16),
            pltpu.VMEM((ROWS, HEAD_DIM), bf16),
            pltpu.VMEM((ROWS, HEAD_DIM), bf16),
            pltpu.VMEM((NX, GROUPS * PIECE, WIDTH), bf16),
            pltpu.VMEM((NX, GROUPS * PIECE, WIDTH), bf16),
            pltpu.VMEM((GROUPS, ZROWS, WIDTH), bf16),
            pltpu.VMEM((NX, GROUPS, ROWS, WIDTH), bf16),
            pltpu.VMEM((GROUPS, FEATS, ROWS), bf16),
            pltpu.VMEM((NX, FEATS, WIDTH), jnp.float32),
            dma((6,)),
            dma((3, NY)), dma((3, NY)),
            dma((GROUPS,)), dma((GROUPS,)),
            dma((4, GROUPS)), dma((4, GROUPS)),
            dma((4, GROUPS)), dma((4, GROUPS)),
            dma((8,)), dma((8,)),
            dma((8,)), dma((8,)),
        ],
        compiler_params=pltpu.CompilerParams(
            collective_id=0, has_side_effects=True, vmem_limit_bytes=60 * 1024 * 1024
        ),
        cost_estimate=pl.CostEstimate(
            flops=2 * 48 * 128 * 512 * 512, bytes_accessed=4 * 1024 * 1024, transcendentals=12 * 128 * 128
        ),
    )(lengths, order, query, keys, values, out_grad)
    return summed


def solution(mesh):
    placed = (P("dp", "tensor"), P("dp", None), P("dp", None), P(("dp", "tensor"), None), P(), P())
    return jax.shard_map(
        local, mesh=mesh, in_specs=placed, out_specs=P("dp", "tensor"), check_vma=False
    )
```

time: 101 us -> 86.9 us (0.86)
  the two profiles are of different devices: /device:TPU:2 before, /device:TPU:1 now
where the time goes in v2:
time: 86.9 us; the launch traced here: 86.8 us
  Pallas kernels  84.5 us (97%)
  local copies, waits for them, and re-layouts  2.26 us (3%)
    pallas_call x1, Pallas kernels, local(): pl.pallas_call(kernel, out_shape=jax.ShapeDtypeStruct((NX * WIDTH, FEATS)...  84.5 us
    unnamed x1, local copies, waits for them, and re-layouts  2.26 us

profile of v2, /device:TPU:1, one launch (start us, length us, event | category | flops | bytes accessed | tf_op | source)
XLA Modules:
  0.0 86.8 jit_solution(6022506621275062406)
XLA Ops:
  0.0 84.5 %shard_map.64 = f32[512,512]{1,0:T(8,128)} custom-call(s32[48]{0:T(128)} %lengths_hbm.1, s32[48]{0:T(128)} %order_hbm.1, bf16[384,512]{1,0:T(8,128)(2,1)} %q_hbm.1, bf16[384,1024]{1,0:T(8,128)(2,1)} %k_hbm.1, bf16[384,1024]{1,0:T(8,128)(2,1)} %v_hbm.1, bf16[24,8192]{1,0:T(8,128)(2,1)} %g_hbm.1), custom_call_target="tpu_custom_call" | custom-call | flops 3221225472 | bytes 4194304 | tf_op jit(solution)/shard_map/pallas_call | solution.py:335
  84.6 2.3 %copy.8 = f32[512,512]{1,0:T(8,128)} copy(f32[512,512]{1,0:T(8,128)} %shard_map.64) | data formatting | bytes 2097152

commit v3 on v2

--- a/solution.py
+++ b/solution.py
@@ -24,22 +24,23 @@
 WIDTH = 128
 FEATS = 512
 PARTS = (0, 2, 1, 3)
-X_FIRST = (0, 1, 2)
-DIRECT = (3, 4, 5, 6)
+X_FIRST = (0, 1, 2, 3)
+DIRECT = ()
 ORDER = (
-    ("xo", 0), ("xo", 1), ("xo", 2), ("zo", 3), ("zo", 8), ("zo", 12), ("zo", 4), ("xp", 0),
-    ("zo", 9), ("zo", 5), ("xp", 1), ("xp", 2), ("zo", 6), ("zp", 8), ("zo", 7), ("xo", 3),
-    ("zp", 12), ("zo", 10), ("A", 0), ("zp", 9), ("zo", 11), ("xo", 4), ("xp", 3), ("xo", 5),
-    ("xo", 8), ("xp", 4), ("xo", 6), ("zp", 7), ("zo", 13), ("zp", 10), ("zo", 14), ("xp", 5),
-    ("xo", 12), ("A", 2), ("A", 6), ("c3", 4), ("c3", 5), ("xp", 8), ("c1", 4), ("xp", 6),
-    ("c1", 5), ("A", 1), ("c3", 3), ("xp", 12), ("xo", 9), ("zp", 11), ("zo", 15), ("c1", 3),
-    ("xo", 7), ("A", 4), ("c3", 8), ("zp", 13), ("zo", 0), ("c1", 8), ("xo", 10), ("c3", 12),
-    ("zp", 14), ("zo", 1), ("c1", 12), ("zp", 15), ("xp", 9), ("xo", 11), ("zo", 2), ("c3", 9),
-    ("xp", 7), ("xo", 13), ("A", 3), ("A", 7), ("c3", 6), ("c1", 6), ("xp", 10), ("c3", 7),
-    ("zp", 0), ("xo", 14), ("c1", 9), ("xp", 11), ("c1", 7), ("zp", 1), ("xo", 15), ("xp", 13),
-    ("c3", 13), ("A", 5), ("c3", 10), ("c1", 10), ("c3", 11), ("zp", 2), ("xp", 14), ("c3", 14),
-    ("c1", 11), ("c4", 0), ("xp", 15), ("c3", 15), ("c1", 13), ("c1", 14), ("c4", 1), ("c4", 2),
-    ("c1", 15),
+    ("T", 0), ("T", 1), ("T", 2), ("P", 0), ("P", 2), ("P", 1), ("P", 3), ("xo", 0),
+    ("xo", 1), ("xo", 2), ("xo", 3), ("zo", 8), ("zo", 12), ("zo", 4), ("xp", 0), ("zo", 9),
+    ("xp", 1), ("xp", 2), ("xp", 3), ("zp", 8), ("zo", 5), ("zp", 12), ("zo", 6), ("Az", 0),
+    ("Ay", 0), ("Ao", 0), ("A", 0), ("zp", 4), ("zo", 7), ("zp", 9), ("zo", 10), ("xo", 8),
+    ("zp", 5), ("zo", 11), ("xo", 12), ("zp", 6), ("zo", 13), ("xp", 8), ("xp", 12), ("A", 2),
+    ("A", 6), ("c3", 12), ("Ay", 1), ("Ao", 1), ("A", 1), ("c1", 12), ("xo", 4), ("zp", 7),
+    ("zo", 14), ("xo", 9), ("zp", 10), ("zo", 15), ("xo", 5), ("zp", 11), ("zo", 0), ("xp", 4),
+    ("xo", 6), ("c3", 4), ("zp", 13), ("zo", 1), ("A", 4), ("c3", 8), ("xp", 9), ("zp", 14),
+    ("xo", 7), ("zo", 2), ("c1", 8), ("c3", 9), ("xp", 5), ("zp", 15), ("xo", 10), ("zo", 3),
+    ("c3", 5), ("c1", 4), ("xp", 6), ("xo", 11), ("c1", 9), ("zp", 0), ("A", 3), ("A", 7),
+    ("c3", 6), ("xp", 7), ("xo", 13), ("c3", 7), ("c1", 5), ("zp", 1), ("xp", 10), ("xo", 14),
+    ("c1", 6), ("xp", 11), ("c1", 7), ("A", 5), ("c3", 10), ("zp", 2), ("xo", 15), ("c3", 11),
+    ("xp", 13), ("c3", 13), ("c1", 10), ("zp", 3), ("xp", 14), ("c3", 14), ("c1", 11), ("c4", 0),
+    ("xp", 15), ("c3", 15), ("c1", 13), ("c4", 1), ("c1", 14), ("c4", 2), ("c1", 15), ("c4", 3),
 )
 MESH = pl.DeviceIdType.MESH
 
@@ -112,33 +113,33 @@
 
     pl.semaphore_wait(barrier, len(peers))
 
-    sends = []
-
     def go(copy):
         copy.start()
-        sends.append(copy)
 
     def x0_rows(dy):
         return pl.ds(dy * 4 * PIECE, 4 * PIECE)
 
-    for dy in PARTS:
+    def x0_start(dy):
         for s in (1, 2, 3):
             go(remote(
                 pk.at[at_x(s), x0_rows(dy)], r0.at[x, x0_rows(dy)],
-                x0_send.at[s - 1, dy], x0_recv.at[s - 1, dy], dev_x(s),
+                x0_send, x0_recv.at[s - 1, dy], dev_x(s),
             ))
+
+    for dy in PARTS:
+        x0_start(dy)
     r0[x] = pk[x]
     acc[...] = jnp.zeros_like(acc)
-
     k_copy.wait()
     v_copy.wait()
     q_copy.wait()
     l_copy.wait()
     o_copy.wait()
+
     key_index = lax.broadcasted_iota(jnp.int32, (SLOT_LEN, SLOT_LEN), 0)
     row_index = lax.broadcasted_iota(jnp.int32, (SLOT_LEN, SLOT_LEN), 1)
     scale = 1.0 / math.sqrt(HEAD_DIM)
-    for s in range(SLOTS):
+    def attend(s):
         length = lengths_ref[order_ref[d * SLOTS + s]]
         rows = slice(s * SLOT_LEN, (s + 1) * SLOT_LEN)
         allowed = (key_index <= row_index) & (key_index < length)
@@ -159,21 +160,21 @@
             att[0, feats, rows] = jnp.where(live, mixed, 0.0).astype(jnp.bfloat16)
 
     def a_copy(src, dst, n, dy, dz):
-        return remote(att.at[2 * src], att.at[2 * dst], a_send.at[n], a_recv.at[dst], dev_dp(dy, dz, 0))
+        return remote(att.at[2 * src], att.at[2 * dst], a_send, a_recv.at[dst], dev_dp(dy, dz, 0))
 
     def b_copy(q):
-        return remote(att.at[2 * q], att.at[2 * q + 1], b_send.at[q], b_recv.at[q], dev_dp(0, 0, 1))
+        return remote(att.at[2 * q], att.at[2 * q + 1], b_send, b_recv.at[q], dev_dp(0, 0, 1))
 
     def a_wait(q):
         a_copy(q, q, 0, 0, 1).wait_recv()
 
     own_rows = pl.ds(pl.multiple_of(zh * ZROWS, ZROWS), ZROWS)
 
-    for dy in PARTS:
+    def dp_part(dy):
         for s in (1, 2, 3):
             remote(
                 pk.at[x, x0_rows(dy)], r0.at[at_x(-s), x0_rows(dy)],
-                x0_send.at[s - 1, dy], x0_recv.at[s - 1, dy], dev_x(s),
+                x0_send, x0_recv.at[s - 1, dy], dev_x(s),
             ).wait_recv()
         for i in range(dy * 4, dy * 4 + 4, 2):
             parts = [r0[xb, i * PIECE : (i + 2) * PIECE, :].astype(jnp.float32) for xb in range(NX)]
@@ -186,10 +187,10 @@
                 continue
             dz, dc = (i // 2) % 2, i % 2
             j = ((NY - dy) % NY) * 4 + dz * 2 + dc
-            go(remote(s1.at[i], gx.at[x, j, own_rows], d_send.at[i], d_recv.at[j], dev_dp(dy, dz, dc)))
+            go(remote(s1.at[i], gx.at[x, j, own_rows], d_send, d_recv.at[j], dev_dp(dy, dz, dc)))
 
     def d_wait(i):
-        remote(s1.at[i], gx.at[x, i, own_rows], d_send.at[i], d_recv.at[i], dev_dp(0, 0, 1)).wait_recv()
+        remote(s1.at[i], gx.at[x, i, own_rows], d_send, d_recv.at[i], dev_dp(0, 0, 1)).wait_recv()
 
     def rows_of(start, size, kind):
         if kind < 2:
@@ -214,13 +215,13 @@
             held = (-1, 1, 2, 2)[kind] if arriving else (0, 0, -1, 1)[kind]
             step = (1, -1, 1, -1)[kind]
         part = z_piece(i, held, kind)
-        return remote(part, part, z_send.at[kind, i], z_recv.at[kind, i], dev_z(step))
+        return remote(part, part, z_send.at[0 if i in X_FIRST else 1], z_recv.at[kind, i], dev_z(step))
 
     def x_ring(i, kind, arriving):
         held = (-1, 1, 2, 2)[kind] if arriving else (0, 0, -1, 1)[kind]
         step = (1, -1, 1, -1)[kind]
         part = x_piece(i, held, kind)
-        return remote(part, part, x_send.at[kind, i], x_recv.at[kind, i], dev_x(step))
+        return remote(part, part, x_send.at[0 if i in X_FIRST else 1], x_recv.at[kind, i], dev_x(step))
 
     def add_block(xb, i):
         total = None
@@ -259,23 +260,30 @@
         for kind in range(3 if i in DIRECT else 4):
             need("z", i, kind)
 
+    def need_a(q):
+        if q > 0:
+            need("a", q)
+
     def need_d(i):
         if i > 0:
             need("d", i)
 
     def step(kind, i):
-        if kind == "A":
-            if i == 0:
-                go(a_copy(0, 1, 0, 0, 1))
-                go(a_copy(0, 6, 1, 1, 0))
-                go(a_copy(0, 2, 2, 3, 0))
-                go(a_copy(0, 4, 6, 2, 0))
-            else:
-                need("a", i)
-            if i == 1:
-                go(a_copy(1, 7, 3, 1, 0))
-                go(a_copy(1, 3, 4, 3, 0))
-                go(a_copy(1, 5, 5, 2, 0))
+        if kind == "P":
+            dp_part(i)
+        elif kind == "T":
+            attend(i)
+        elif kind == "Az":
+            go(a_copy(0, 1, 0, 0, 1))
+        elif kind == "Ay":
+            need_a(i)
+            go(a_copy(i, 6 + i, 1 + 3 * i, 1, 0))
+            go(a_copy(i, 2 + i, 2 + 3 * i, 3, 0))
+        elif kind == "Ao":
+            need_a(i)
+            go(a_copy(i, 4 + i, 3 + 3 * i, 2, 0))
+        elif kind == "A":
+            need_a(i)
             go(b_copy(i))
         elif kind == "zo":
             if i in X_FIRST:
@@ -323,8 +331,18 @@
     for xb in range(NX):
         out_ref[xb * WIDTH : (xb + 1) * WIDTH, :] = acc[xb].T * (1.0 / (GROUPS * ROWS))
 
-    for copy in sends:
-        copy.wait_send()
+    nx, nz = len(X_FIRST), GROUPS - len(X_FIRST)
+    for sem, ref in (
+        (x0_send, pk.at[0:3]),
+        (d_send, s1.at[1:GROUPS]),
+        (a_send, att.at[0:7]),
+        (b_send, att.at[0:8]),
+        (x_send.at[0], gx.at[0:3, 0:nx, 0:ZROWS]),
+        (x_send.at[1], gx.at[0:3, 0:nz]),
+        (z_send.at[0], gx.at[0:3, 0:nx]),
+        (z_send.at[1], gx.at[0:3, 0:nz, 0:ZROWS]),
+    ):
+        remote(ref, ref, sem, d_recv.at[0], dev_x(1)).wait_send()
 
 
 def local(query, keys, values, out_grad, lengths, order):
@@ -351,12 +369,12 @@
             pltpu.VMEM((GROUPS, FEATS, ROWS), bf16),
             pltpu.VMEM((NX, FEATS, WIDTH), jnp.float32),
             dma((6,)),
-            dma((3, NY)), dma((3, NY)),
-            dma((GROUPS,)), dma((GROUPS,)),
-            dma((4, GROUPS)), dma((4, GROUPS)),
-            dma((4, GROUPS)), dma((4, GROUPS)),
-            dma((8,)), dma((8,)),
-            dma((8,)), dma((8,)),
+            dma, dma((3, NY)),
+            dma, dma((GROUPS,)),
+            dma((2,)), dma((4, GROUPS)),
+            dma((2,)), dma((4, GROUPS)),
+            dma, dma((8,)),
+            dma, dma((8,)),
         ],
         compiler_params=pltpu.CompilerParams(
             collective_id=0, has_side_effects=True, vmem_limit_bytes=60 * 1024 * 1024

time: 86.9 us -> 82.2 us (0.946)
  the two profiles are of different devices: /device:TPU:1 before, /device:TPU:2 now
where the time goes in v3:
time: 82.2 us; the launch traced here: 80.6 us
  Pallas kernels  78.3 us (95%)
  local copies, waits for them, and re-layouts  2.26 us (3%)
    pallas_call x1, Pallas kernels, local(): pl.pallas_call(kernel, out_shape=jax.ShapeDtypeStruct((NX * WIDTH, FEATS)...  78.3 us
    unnamed x1, local copies, waits for them, and re-layouts  2.26 us

profile of v3, /device:TPU:2, one launch (start us, length us, event | category | flops | bytes accessed | tf_op | source)
XLA Modules:
  0.0 80.6 jit_solution(309271647037560388)
XLA Ops:
  0.0 78.3 %shard_map.64 = f32[512,512]{1,0:T(8,128)} custom-call(s32[48]{0:T(128)} %lengths_hbm.1, s32[48]{0:T(128)} %order_hbm.1, bf16[384,512]{1,0:T(8,128)(2,1)} %q_hbm.1, bf16[384,1024]{1,0:T(8,128)(2,1)} %k_hbm.1, bf16[384,1024]{1,0:T(8,128)(2,1)} %v_hbm.1, bf16[24,8192]{1,0:T(8,128)(2,1)} %g_hbm.1), custom_call_target="tpu_custom_call" | custom-call | flops 3221225472 | bytes 4194304 | tf_op jit(solution)/shard_map/pallas_call | solution.py:353
  78.3 2.3 %copy.8 = f32[512,512]{1,0:T(8,128)} copy(f32[512,512]{1,0:T(8,128)} %shard_map.64) | data formatting | bytes 2097152

commit v4 on v3

--- a/solution.py
+++ b/solution.py
@@ -24,23 +24,24 @@
 WIDTH = 128
 FEATS = 512
 PARTS = (0, 2, 1, 3)
-X_FIRST = (0, 1, 2, 3)
+X_FIRST = (0, 1, 2)
 DIRECT = ()
 ORDER = (
     ("T", 0), ("T", 1), ("T", 2), ("P", 0), ("P", 2), ("P", 1), ("P", 3), ("xo", 0),
-    ("xo", 1), ("xo", 2), ("xo", 3), ("zo", 8), ("zo", 12), ("zo", 4), ("xp", 0), ("zo", 9),
-    ("xp", 1), ("xp", 2), ("xp", 3), ("zp", 8), ("zo", 5), ("zp", 12), ("zo", 6), ("Az", 0),
-    ("Ay", 0), ("Ao", 0), ("A", 0), ("zp", 4), ("zo", 7), ("zp", 9), ("zo", 10), ("xo", 8),
-    ("zp", 5), ("zo", 11), ("xo", 12), ("zp", 6), ("zo", 13), ("xp", 8), ("xp", 12), ("A", 2),
-    ("A", 6), ("c3", 12), ("Ay", 1), ("Ao", 1), ("A", 1), ("c1", 12), ("xo", 4), ("zp", 7),
-    ("zo", 14), ("xo", 9), ("zp", 10), ("zo", 15), ("xo", 5), ("zp", 11), ("zo", 0), ("xp", 4),
-    ("xo", 6), ("c3", 4), ("zp", 13), ("zo", 1), ("A", 4), ("c3", 8), ("xp", 9), ("zp", 14),
-    ("xo", 7), ("zo", 2), ("c1", 8), ("c3", 9), ("xp", 5), ("zp", 15), ("xo", 10), ("zo", 3),
-    ("c3", 5), ("c1", 4), ("xp", 6), ("xo", 11), ("c1", 9), ("zp", 0), ("A", 3), ("A", 7),
-    ("c3", 6), ("xp", 7), ("xo", 13), ("c3", 7), ("c1", 5), ("zp", 1), ("xp", 10), ("xo", 14),
-    ("c1", 6), ("xp", 11), ("c1", 7), ("A", 5), ("c3", 10), ("zp", 2), ("xo", 15), ("c3", 11),
-    ("xp", 13), ("c3", 13), ("c1", 10), ("zp", 3), ("xp", 14), ("c3", 14), ("c1", 11), ("c4", 0),
-    ("xp", 15), ("c3", 15), ("c1", 13), ("c4", 1), ("c1", 14), ("c4", 2), ("c1", 15), ("c4", 3),
+    ("xo", 1), ("Ay", 0), ("A", 0), ("xo", 2), ("zo", 3), ("zo", 8), ("zo", 12), ("zo", 4),
+    ("xp", 0), ("xp", 1), ("xp", 2), ("zp", 3), ("zo", 5), ("zp", 8), ("zo", 6), ("Az", 0),
+    ("zp", 12), ("zo", 7), ("zp", 4), ("zo", 9), ("xo", 3), ("zp", 5), ("zo", 10), ("xo", 8),
+    ("Az", 1), ("zp", 6), ("zo", 11), ("A", 6), ("A", 2), ("Ap", 0), ("xp", 3), ("xo", 12),
+    ("zp", 7), ("zo", 13), ("Az", 2), ("xo", 4), ("xp", 8), ("zp", 9), ("zo", 14), ("xo", 5),
+    ("zp", 10), ("zo", 15), ("Ap", 1), ("xp", 12), ("c3", 12), ("Az", 3), ("xo", 6), ("A", 4),
+    ("xp", 4), ("c3", 4), ("zp", 11), ("xo", 7), ("zo", 0), ("zp", 13), ("zo", 1), ("c3", 8),
+    ("xp", 5), ("Ap", 2), ("c3", 5), ("xo", 9), ("c1", 8), ("c1", 12), ("zp", 14), ("zo", 2),
+    ("xp", 6), ("xo", 10), ("zp", 15), ("c1", 4), ("Ap", 3), ("xp", 7), ("xo", 11), ("A", 1),
+    ("c1", 5), ("xp", 9), ("c3", 9), ("zp", 0), ("c3", 3), ("xo", 13), ("A", 3), ("A", 7),
+    ("c1", 3), ("xp", 10), ("A", 5), ("c3", 6), ("zp", 1), ("xp", 11), ("xo", 14), ("c1", 6),
+    ("c3", 7), ("c1", 7), ("c1", 9), ("c3", 10), ("xp", 13), ("c3", 11), ("zp", 2), ("xo", 15),
+    ("c1", 10), ("c1", 11), ("c3", 13), ("c4", 0), ("xp", 14), ("c1", 13), ("c3", 14), ("c4", 1),
+    ("xp", 15), ("c3", 15), ("c1", 14), ("c4", 2), ("c1", 15),
 )
 MESH = pl.DeviceIdType.MESH
 
@@ -159,14 +160,19 @@
             mixed = jnp.dot(values_t, probs, preferred_element_type=jnp.float32)
             att[0, feats, rows] = jnp.where(live, mixed, 0.0).astype(jnp.bfloat16)
 
-    def a_copy(src, dst, n, dy, dz):
-        return remote(att.at[2 * src], att.at[2 * dst], a_send, a_recv.at[dst], dev_dp(dy, dz, 0))
+    def a_copy(src, dst, dy, dz, head=None):
+        part = slice(0, FEATS) if head is None else slice(head * HEAD_DIM, (head + 1) * HEAD_DIM)
+        return remote(
+            att.at[2 * src, part], att.at[2 * dst, part], a_send, a_recv.at[dst, head or 0], dev_dp(dy, dz, 0)
+        )
 
     def b_copy(q):
         return remote(att.at[2 * q], att.at[2 * q + 1], b_send, b_recv.at[q], dev_dp(0, 0, 1))
 
     def a_wait(q):
-        a_copy(q, q, 0, 0, 1).wait_recv()
+        for head in range(FEATS // HEAD_DIM) if q % 2 else (None,):
+            if q > 1:
+                a_copy(q, q, 0, 1, head).wait_recv()
 
     own_rows = pl.ds(pl.multiple_of(zh * ZROWS, ZROWS), ZROWS)
 
@@ -274,14 +280,16 @@
         elif kind == "T":
             attend(i)
         elif kind == "Az":
-            go(a_copy(0, 1, 0, 0, 1))
+            go(a_copy(0, 1, 0, 1, i))
+        elif kind == "Ap":
+            a_copy(1, 1, 0, 1, i).wait_recv()
+            go(a_copy(1, 7, 1, 0, i))
+            go(a_copy(1, 3, 3, 0, i))
+            go(a_copy(1, 5, 2, 0, i))
         elif kind == "Ay":
-            need_a(i)
-            go(a_copy(i, 6 + i, 1 + 3 * i, 1, 0))
-            go(a_copy(i, 2 + i, 2 + 3 * i, 3, 0))
-        elif kind == "Ao":
-            need_a(i)
-            go(a_copy(i, 4 + i, 3 + 3 * i, 2, 0))
+            go(a_copy(0, 6, 1, 0))
+            go(a_copy(0, 2, 3, 0))
+            go(a_copy(0, 4, 2, 0))
         elif kind == "A":
             need_a(i)
             go(b_copy(i))
@@ -373,7 +381,7 @@
             dma, dma((GROUPS,)),
             dma((2,)), dma((4, GROUPS)),
             dma((2,)), dma((4, GROUPS)),
-            dma, dma((8,)),
+            dma, dma((8, 4)),
             dma, dma((8,)),
         ],
         compiler_params=pltpu.CompilerParams(

time: 82.2 us -> 80.6 us (0.981)
  Pallas kernels: 78.3 us -> 76.7 us
    pallas_call x1, Pallas kernels: 78.3 us -> 76.7 us  [local(): pl.pallas_call(kernel, out_shape=jax.ShapeDtypeStruct((NX * WIDTH, FEATS)...]
where the time goes in v4:
time: 80.6 us; the launch traced here: 79 us
  Pallas kernels  76.7 us (95%)
  local copies, waits for them, and re-layouts  2.26 us (3%)
    pallas_call x1, Pallas kernels, local(): pl.pallas_call(kernel, out_shape=jax.ShapeDtypeStruct((NX * WIDTH, FEATS)...  76.7 us
    unnamed x1, local copies, waits for them, and re-layouts  2.26 us

profile of v4, /device:TPU:2, one launch (start us, length us, event | category | flops | bytes accessed | tf_op | source)
XLA Modules:
  0.0 79.0 jit_solution(3564747960193219547)
XLA Ops:
  0.0 76.7 %shard_map.64 = f32[512,512]{1,0:T(8,128)} custom-call(s32[48]{0:T(128)} %lengths_hbm.1, s32[48]{0:T(128)} %order_hbm.1, bf16[384,512]{1,0:T(8,128)(2,1)} %q_hbm.1, bf16[384,1024]{1,0:T(8,128)(2,1)} %k_hbm.1, bf16[384,1024]{1,0:T(8,128)(2,1)} %v_hbm.1, bf16[24,8192]{1,0:T(8,128)(2,1)} %g_hbm.1), custom_call_target="tpu_custom_call" | custom-call | flops 3221225472 | bytes 4194304 | tf_op jit(solution)/shard_map/pallas_call | solution.py:361
  76.8 2.3 %copy.8 = f32[512,512]{1,0:T(8,128)} copy(f32[512,512]{1,0:T(8,128)} %shard_map.64) | data formatting | bytes 2097152

commit v5 on v4

--- a/solution.py
+++ b/solution.py
@@ -82,7 +82,7 @@
         )
 
     barrier = pltpu.get_barrier_semaphore()
-    peers = [dev_x(s) for s in (1, 2, 3)] + [dev_z(s) for s in (1, 2, 3)]
+    peers = [dev_x(s) for s in (1, 2, 3)] + [dev_z(1), dev_z(-1)]
     peers += [dev_dp(i // 4, (i // 2) % 2, i % 2) for i in range(1, GROUPS)]
     for peer in peers:
         pl.semaphore_signal(barrier, inc=1, device_id=peer, device_id_type=MESH)
@@ -238,12 +238,22 @@
             total = square if total is None else total + square
         acc[xb] += total
 
+    def add_pair(xa, xb, i):
+        total = None
+        for s in range(SLOTS):
+            rows = slice(s * SLOT_LEN, (s + 1) * SLOT_LEN)
+            grads = jnp.concatenate([gx[xa, i, rows, :], gx[xb, i, rows, :]], axis=1)
+            gradient = jnp.dot(att[i, :, rows], grads, preferred_element_type=jnp.float32)
+            square = gradient * gradient
+            total = square if total is None else total + square
+        acc[xa] += total[:, :WIDTH]
+        acc[xb] += total[:, WIDTH:]
+
     def add_blocks(i, first, count):
-        def body(n, carry):
-            add_block((x + first + n) % NX, i)
-            return carry
-
-        lax.fori_loop(0, count, body, 0)
+        if count % 2:
+            add_block((x + first) % NX, i)
+        for n in range(count % 2, count, 2):
+            add_pair((x + first + n) % NX, (x + first + n + 1) % NX, i)
 
     waited = set()
 

time: 80.6 us -> 80.2 us (level)
  no operation moved by 1% of the time
where the time goes in v5:
time: 80.2 us; the launch traced here: 79 us
  Pallas kernels  76.7 us (96%)
  local copies, waits for them, and re-layouts  2.26 us (3%)
    pallas_call x1, Pallas kernels, local(): pl.pallas_call(kernel, out_shape=jax.ShapeDtypeStruct((NX * WIDTH, FEATS)...  76.7 us
    unnamed x1, local copies, waits for them, and re-layouts  2.26 us

profile of v5, /device:TPU:2, one launch (start us, length us, event | category | flops | bytes accessed | tf_op | source)
XLA Modules:
  0.0 79.0 jit_solution(18180111110170769040)
XLA Ops:
  0.0 76.7 %shard_map.64 = f32[512,512]{1,0:T(8,128)} custom-call(s32[48]{0:T(128)} %lengths_hbm.1, s32[48]{0:T(128)} %order_hbm.1, bf16[384,512]{1,0:T(8,128)(2,1)} %q_hbm.1, bf16[384,1024]{1,0:T(8,128)(2,1)} %k_hbm.1, bf16[384,1024]{1,0:T(8,128)(2,1)} %v_hbm.1, bf16[24,8192]{1,0:T(8,128)(2,1)} %g_hbm.1), custom_call_target="tpu_custom_call" | custom-call | flops 3221225472 | bytes 4194304 | tf_op jit(solution)/shard_map/pallas_call | solution.py:371
  76.7 2.3 %copy.8 = f32[512,512]{1,0:T(8,128)} copy(f32[512,512]{1,0:T(8,128)} %shard_map.64) | data formatting | bytes 2097152
